TPU v7x, 512 devices: a whole 4x4x16 slice. The times are simulated.
512 devices in a mesh: dp: 16 (over z_lo, core), tm: 32 (over x, y, z_hi).
Axes of the slice: x: 4, y: 4, z: 16 (z_hi: 2, z_lo: 8; z = z_hi * 8 + z_lo), core: 2. Of those that a mesh axis runs over, the one named last changes fastest.
Arguments:
- queries: bfloat16 [16, 8192, 1152], P('dp', 'tm'), may hold values from -96 to 96
- keys: bfloat16 [16, 8192, 1152], P('dp', 'tm'), may hold values from -6 to 6
- values: bfloat16 [16, 8192, 1152], P('dp', 'tm'), may hold values from -6 to 6
- out_grad: bfloat16 [16, 8192, 1152], P('dp', 'tm'), may hold values from -6 to 6
- lengths: int32 [16], P('dp'), may hold values from 2048 to 8192, as said below
- rel_bias: float32 [12, 768], replicated, may hold values from -4 to 4
Outputs:
- query_grad: bfloat16 [16, 8192, 1152], P('dp', 'tm')
- key_grad: bfloat16 [16, 8192, 1152], P('dp', 'tm')
- value_grad: bfloat16 [16, 8192, 1152], P('dp', 'tm')
- bias_grad: float32 [12, 768], replicated
Inputs may be any that keep to these rules, and one draw needn't show every extreme that they name: Every recording's valid frames are its first lengths[r] frames; some recording is valid to its end.
All inputs are finite; a program needn't handle non-finite values.
Results may differ from a plain program's by a relative error of at most 0.007.
Values may be sent and summed in bfloat16 or wider, within the bound.
A program may use at most 128 MiB of HBM per device.

v0:
```python
import jax
import jax.numpy as jnp
from jax import lax
from jax.experimental import pallas as pl
from jax.experimental.pallas import tpu as pltpu
from jax.sharding import PartitionSpec as P

MESH = pl.DeviceIdType.MESH
MASKED = -1000000000.0
BLOCK = 256
HEAD = 96
GROUP = 4
WIDE = GROUP * HEAD
WINDOWS = ((0, 128), (0, 256), (128, 256), (256, 128))
SCALING = HEAD ** (-0.5)


def nt(a, b):
    return lax.dot_general(a, b, (((1,), (1,)), ((), ())), preferred_element_type=jnp.float32)


def nn(a, b):
    return jnp.dot(a, b, preferred_element_type=jnp.float32)


def head_lanes(j):
    start, width = WINDOWS[j]
    lane = lax.broadcasted_iota(jnp.int32, (1, width), 1) + start
    return ((lane >= HEAD * j) & (lane < HEAD * (j + 1))).astype(jnp.float32).astype(jnp.bfloat16)


def reverse_lanes(x):
    rows, width = x.shape
    row = lax.broadcasted_iota(jnp.int32, (128, 128), 0)
    col = lax.broadcasted_iota(jnp.int32, (128, 128), 1)
    flip = (row + col == 127).astype(jnp.float32)
    parts = [
        lax.dot_general(
            x[:, at : at + 128],
            flip,
            (((1,), (0,)), ((), ())),
            preferred_element_type=jnp.float32,
            precision=lax.Precision.HIGHEST,
        )
        for at in range(width - 128, -1, -128)
    ]
    return jnp.concatenate(parts, axis=1)


def diagonal_partials(x):
    x = jnp.concatenate([x, jnp.zeros((BLOCK, 128), jnp.float32)], axis=1)
    x = x.reshape(32, 8, 384)
    for level in range(4):
        pairs = x.reshape(x.shape[0] // 2, 2, 8, 384)
        x = pltpu.roll(pairs[:, 0], 8 << level, 2) + pairs[:, 1]
    zeros = jnp.zeros((8, 128), jnp.float32)
    return jnp.concatenate([zeros, x[0]], axis=1) + jnp.concatenate([x[1], zeros], axis=1)


def kernel(
    length_ref, q_hbm, k_hbm, v_hbm, g_hbm, rel_ref,
    dq_hbm, dk_hbm, dv_hbm, table_ref,
    qbuf, kbuf, vbuf, gbuf, ktr, rq, rg, sdq, rdq,
    expo, dpr, toep, skew, dk_acc, dv_acc, dq_tr, dq_own, gmask,
    st_send, st_recv, bk_send, bk_recv, tops, parts,
    odq, odk, odv,
    load_sem, out_sem, send_sem, recv_sem,
):
    dp = lax.axis_index("dp")
    tm = lax.axis_index("tm")
    count = lax.axis_size("tm")
    before = {"dp": dp, "tm": lax.rem(tm + count - 1, count)}
    after = {"dp": dp, "tm": lax.rem(tm + 1, count)}
    heads = rel_ref.shape[0]
    groups = heads // GROUP

    def lanes(g):
        return pl.ds(pl.multiple_of(g * WIDE, 128), WIDE)

    def remote(src, dst, kind, g, target):
        return pltpu.make_async_remote_copy(
            src_ref=src, dst_ref=dst.at[g],
            send_sem=send_sem.at[kind, g], recv_sem=recv_sem.at[kind, g],
            device_id=target, device_id_type=MESH,
        )

    def send_q(g):
        return remote(q_hbm.at[0, :, lanes(g)], rq, 0, g, before)

    def send_g(g):
        return remote(g_hbm.at[0, :, lanes(g)], rg, 1, g, before)

    def send_stats(g):
        return remote(st_send.at[g], st_recv, 2, g, before)

    def send_back(g):
        return remote(bk_send.at[g], bk_recv, 3, g, after)

    def send_dq(g):
        return remote(sdq.at[g], rdq, 4, g, after)

    def load(n, src, dst, g):
        return pltpu.make_async_copy(src.at[0, :, lanes(g)], dst.at[g], load_sem.at[n, g])

    def store(n, src, dst, g):
        return pltpu.make_async_copy(src.at[g], dst.at[0, :, lanes(g)], out_sem.at[n, g])

    loads = [
        load(n, src, dst, g)
        for g in range(groups)
        for n, (src, dst) in enumerate(((q_hbm, qbuf), (k_hbm, kbuf), (v_hbm, vbuf), (g_hbm, gbuf)))
    ]
    for copy in loads:
        copy.start()

    barrier = pltpu.get_barrier_semaphore()
    for neighbour in (before, after):
        pl.semaphore_signal(barrier, inc=1, device_id=neighbour, device_id_type=MESH)
    pl.semaphore_wait(barrier, 2)
    send_q(0).start()
    send_g(0).start()

    length = length_ref[0]
    live_keys = length - tm * BLOCK
    live_cross = jnp.where(tm == count - 1, 0, live_keys)
    live_next = jnp.where(tm == count - 1, 0, live_keys - BLOCK)

    flipped = pltpu.roll(reverse_lanes(rel_ref[...]), 3 * BLOCK - 1, 1)
    spread = jnp.broadcast_to(flipped[:, None, :], (heads, 8, 3 * BLOCK))
    sub = lax.broadcasted_iota(jnp.int32, (heads, 8, 3 * BLOCK), 1)
    for bit in (1, 2, 4):
        spread = jnp.where(((7 - sub) & bit) != 0, pltpu.roll(spread, 3 * BLOCK - bit, 2), spread)
    skew[...] = spread

    def build(h, carry):
        base = skew[h]
        for a in range(BLOCK // 8):
            shift = 8 * (BLOCK // 8 - 1 - a)
            turned = base if shift == 0 else pltpu.roll(base, 3 * BLOCK - shift, 1)
            toep[h, 8 * a : 8 * a + 8, :] = turned[:, : 2 * BLOCK]
        return carry

    lax.fori_loop(0, heads, build, 0)
    for copy in loads:
        copy.wait()

    key_row = lax.broadcasted_iota(jnp.int32, (BLOCK, BLOCK), 0)
    frame_row = lax.broadcasted_iota(jnp.int32, (BLOCK, WIDE), 0)

    def own_stats(g, carry):
        live = frame_row < live_keys
        gbuf[g] = jnp.where(live, gbuf[g].astype(jnp.float32), 0.0).astype(jnp.bfloat16)
        ktr[g] = kbuf[g].T
        for j in range(GROUP):
            h = g * GROUP + j
            start, width = WINDOWS[j]
            window = slice(start, start + width)
            mask = head_lanes(j)
            scores = nt(kbuf[g, :, window] * mask, qbuf[g, :, window]) * SCALING
            scores = scores + toep[h, :, :BLOCK]
            scores = jnp.where(key_row < live_keys, scores, MASKED)
            top = jnp.max(scores, axis=0, keepdims=True)
            e = jnp.exp(scores - top)
            dprobs = nt(vbuf[g, :, window] * mask, gbuf[g, :, window])
            total = jnp.sum(e, axis=0, keepdims=True)
            mixed = jnp.sum(e * dprobs, axis=0, keepdims=True)
            expo[h] = e
            dpr[h] = dprobs
            tops[g, j : j + 1, :] = top
            st_send[g, j : j + 1, :] = top + jnp.log(total)
            st_send[g, GROUP + j : GROUP + j + 1, :] = mixed / total
        send_stats(g).start()
        return carry

    lax.fori_loop(0, groups, own_stats, 0)
    for g in range(1, groups):
        send_q(g).start()
        send_g(g).start()

    def cross(g, carry):
        send_q(g).wait_recv()
        send_g(g).wait_recv()
        send_stats(g).wait_recv()

        @pl.when(g > 0)
        def _():
            send_dq(g - 1).start()

        gmask[...] = jnp.where(
            frame_row < live_next, rg[g].astype(jnp.float32), 0.0
        ).astype(jnp.bfloat16)
        dk_acc[g] = jnp.zeros((BLOCK, WIDE), jnp.float32)
        dv_acc[g] = jnp.zeros((BLOCK, WIDE), jnp.float32)
        for j in range(GROUP):
            h = g * GROUP + j
            start, width = WINDOWS[j]
            window = slice(start, start + width)
            mask = head_lanes(j)
            scores = nt(kbuf[g, :, window] * mask, rq[g, :, window]) * SCALING
            scores = scores + toep[h, :, BLOCK:]
            scores = jnp.where(key_row < live_cross, scores, MASKED)
            top = jnp.max(scores, axis=0, keepdims=True)
            e = jnp.exp(scores - top)
            dprobs = nt(vbuf[g, :, window] * mask, gmask[:, window])
            total = jnp.sum(e, axis=0, keepdims=True)
            mixed = jnp.sum(e * dprobs, axis=0, keepdims=True)
            lse_here = top + jnp.log(total)
            lse_there = st_recv[g, j : j + 1, :]
            highest = jnp.maximum(lse_here, lse_there)
            here = jnp.exp(lse_here - highest)
            there = jnp.exp(lse_there - highest)
            both = here + there
            lse = highest + jnp.log(both)
            delta = (here * (mixed / total) + there * st_recv[g, GROUP + j : GROUP + j + 1, :]) / both
            bk_send[g, j : j + 1, :] = lse
            bk_send[g, GROUP + j : GROUP + j + 1, :] = delta
            probs = e * jnp.exp(top - lse)
            dscores = probs * (dprobs - delta)
            probs_b = probs.astype(jnp.bfloat16)
            dscores_b = dscores.astype(jnp.bfloat16)
            dv_acc[g, :, window] += nn(probs_b, gmask[:, window] * mask)
            dk_acc[g, :, window] += nn(dscores_b, rq[g, :, window] * mask)
            dq_tr[HEAD * j : HEAD * (j + 1), :] = nn(ktr[g, HEAD * j : HEAD * (j + 1), :], dscores_b)
            parts[h, :, : BLOCK] = jnp.zeros((8, BLOCK), jnp.float32)
            parts[h, :, BLOCK:] = diagonal_partials(dscores)
        send_back(g).start()
        sdq[g] = (dq_tr[...].T * SCALING).astype(jnp.bfloat16)
        return carry

    lax.fori_loop(0, groups, cross, 0)
    send_dq(groups - 1).start()

    def own_rest(g, carry):
        send_back(g).wait_recv()
        for j in range(GROUP):
            h = g * GROUP + j
            start, width = WINDOWS[j]
            window = slice(start, start + width)
            mask = head_lanes(j)
            probs = expo[h] * jnp.exp(tops[g, j : j + 1, :] - bk_recv[g, j : j + 1, :])
            dscores = probs * (dpr[h] - bk_recv[g, GROUP + j : GROUP + j + 1, :])
            probs_b = probs.astype(jnp.bfloat16)
            dscores_b = dscores.astype(jnp.bfloat16)
            dv_acc[g, :, window] += nn(probs_b, gbuf[g, :, window] * mask)
            dk_acc[g, :, window] += nn(dscores_b, qbuf[g, :, window] * mask)
            dq_tr[HEAD * j : HEAD * (j + 1), :] = nn(ktr[g, HEAD * j : HEAD * (j + 1), :], dscores_b)
            parts[h, :, : 2 * BLOCK] += diagonal_partials(dscores)
        dq_own[g] = dq_tr[...].T * SCALING
        odk[g] = (dk_acc[g] * SCALING).astype(jnp.bfloat16)
        odv[g] = dv_acc[g].astype(jnp.bfloat16)
        store(1, odk, dk_hbm, g).start()
        store(2, odv, dv_hbm, g).start()
        return carry

    lax.fori_loop(0, groups, own_rest, 0)

    folded = parts[...]
    for bit in (1, 2, 4):
        folded = jnp.where(((7 - sub) & bit) != 0, pltpu.roll(folded, bit, 2), folded)
    sums = jnp.sum(folded, axis=1)
    table_ref[...] = pltpu.roll(reverse_lanes(sums), 3 * BLOCK - 1, 1)

    def finish(g, carry):
        send_dq(g).wait_recv()
        odq[g] = (dq_own[g] + rdq[g].astype(jnp.float32)).astype(jnp.bfloat16)
        store(0, odq, dq_hbm, g).start()
        return carry

    lax.fori_loop(0, groups, finish, 0)
    for g in range(groups):
        for copy in (send_q(g), send_g(g), send_stats(g), send_back(g), send_dq(g)):
            copy.wait_send()
        for n, (src, dst) in enumerate(((odq, dq_hbm), (odk, dk_hbm), (odv, dv_hbm))):
            store(n, src, dst, g).wait()


def per_device(queries, keys, values, out_grad, lengths, rel_bias):
    _, frames, width = queries.shape
    heads, offsets = rel_bias.shape
    groups = heads // GROUP
    bf16, f32 = jnp.bfloat16, jnp.float32
    wide = pltpu.VMEM((groups, BLOCK, WIDE), bf16)
    wide32 = pltpu.VMEM((groups, BLOCK, WIDE), f32)
    stats = pltpu.VMEM((groups, 2 * GROUP, BLOCK), f32)
    block = jax.ShapeDtypeStruct((1, frames, width), bf16)
    anywhere = pl.BlockSpec(memory_space=pl.ANY)
    in_vmem = pl.BlockSpec(memory_space=pltpu.VMEM)
    dq, dk, dv, table = pl.pallas_call(
        kernel,
        out_shape=(block, block, block, jax.ShapeDtypeStruct((heads, offsets), f32)),
        in_specs=[pl.BlockSpec(memory_space=pltpu.SMEM)] + [anywhere] * 4 + [in_vmem],
        out_specs=(anywhere, anywhere, anywhere, in_vmem),
        scratch_shapes=[
            wide, wide, wide, wide,
            pltpu.VMEM((groups, WIDE, BLOCK), bf16),
            wide, wide, wide, wide,
            pltpu.VMEM((heads, BLOCK, BLOCK), f32),
            pltpu.VMEM((heads, BLOCK, BLOCK), f32),
            pltpu.VMEM((heads, BLOCK, 2 * BLOCK), f32),
            pltpu.VMEM((heads, 8, offsets), f32),
            wide32, wide32,
            pltpu.VMEM((WIDE, BLOCK), f32),
            wide32,
            pltpu.VMEM((BLOCK, WIDE), bf16),
            stats, stats, stats, stats, stats,
            pltpu.VMEM((heads, 8, offsets), f32),
            wide, wide, wide,
            pltpu.SemaphoreType.DMA((4, groups)),
            pltpu.SemaphoreType.DMA((3, groups)),
            pltpu.SemaphoreType.DMA((5, groups)),
            pltpu.SemaphoreType.DMA((5, groups)),
        ],
        compiler_params=pltpu.CompilerParams(
            collective_id=0, has_side_effects=True, vmem_limit_bytes=48 << 20
        ),
    )(lengths, queries, keys, values, out_grad, rel_bias)
    return dq, dk, dv, lax.psum(table, ("dp", "tm"))


def solution(mesh):
    placed = P("dp", "tm", None)
    return jax.shard_map(
        per_device,
        mesh=mesh,
        in_specs=(placed, placed, placed, placed, P("dp"), P()),
        out_specs=(placed, placed, placed, P()),
        check_vma=False,
    )
```

profile of v0, /device:TPU:1, one launch (start us, length us, event | category | flops | bytes accessed | tf_op | source)
XLA Modules:
  0.0 290.9 jit_solution(8633979735413345605)
XLA Ops:
  1.3 0.0 copy-start
  1.3 1.1 copy-done
  2.3 0.0 copy-start.1
  2.3 1.1 copy-done.1
  3.4 0.0 copy-start.2
  3.4 1.1 copy-done.2
  4.5 0.0 copy-start.3
  4.5 1.1 copy-done.3
  5.5 0.0 copy-start.4
  5.5 0.8 copy-done.4
  6.3 166.3 %shard_map.93 = (bf16[1,256,1152]{2,1,0:T(8,128)(2,1)S(1)}, bf16[1,256,1152]{2,1,0:T(8,128)(2,1)S(1)}, bf16[1,256,1152]{2,1,0:T(8,128)(2,1)S(1)}, f32[12,768]{1,0:T(8,128)S(1)}) custom-call(s32[1]{0:T(128)S(6)} %copy.13.length_ref, bf16[1,256,1152]{2,1,0:T(8,128)(2,1)S(1)} %copy-done, bf16[1,256,1152]{2,1,0:T(8,128)(2,1)S(1)} %copy-done.1, ...), custom_call_target="tpu_custom_call" | custom-call | tf_op jit(solution)/shard_map/pallas_call | solution.py:288
  172.7 115.8 %psum.7 = f32[12,768]{1,0:T(8,128)} all-reduce(f32[12,768]{1,0:T(8,128)S(1)} %get-tuple-element.11), channel_id=1, replica_groups=mesh['dp'=16,'tm'=32] {'dp','tm'}, use_global_device_ids=true, to_apply=%region_0.0 | all-reduce | flops 9216 | bytes 73728 | tf_op jit(solution)/shard_map/psum | solution.py:317
  288.5 0.8 copy.14
  289.3 0.8 copy.15
  290.1 0.8 copy.16
Async XLA Ops:
  1.3 1.1 copy-start
  2.3 1.1 copy-start.1
  3.4 1.1 copy-start.2
  4.5 1.1 copy-start.3
  5.5 0.8 copy-start.4
where the time goes:
time: 291 us
  Pallas kernels  166 us (57%)
  blocking collectives  116 us (40%)
  local copies, waits for them, and re-layouts  7.49 us (3%)
    pallas_call x1, Pallas kernels, per_device(): pl.pallas_call(kernel, out_shape=(block, block, block, jax.ShapeDtypeStru...  166 us
    psum x1, blocking collectives, per_device(): return (dq, dk, dv, lax.psum(table, ('dp', 'tm')))  116 us
    unnamed x13, local copies, waits for them, and re-layouts  7.49 us

commit v1 on v0

--- a/solution.py
+++ b/solution.py
@@ -13,6 +13,10 @@
 WIDE = GROUP * HEAD
 WINDOWS = ((0, 128), (0, 256), (128, 256), (256, 128))
 SCALING = HEAD ** (-0.5)
+NX, NY, NZ_HI, NZ_LO, CORES = 4, 4, 2, 8, 2
+NZ = NZ_HI * NZ_LO
+NEAR = min(4, NZ)
+FAR = NZ // NEAR
 
 
 def nt(a, b):
@@ -57,6 +61,25 @@
     return jnp.concatenate([zeros, x[0]], axis=1) + jnp.concatenate([x[1], zeros], axis=1)
 
 
+def place(dp, tm):
+    return tm // NZ_HI // NY, tm // NZ_HI % NY, (tm % NZ_HI) * NZ_LO + dp // CORES, dp % CORES
+
+
+def device(x, y, z, core):
+    return {"dp": (z % NZ_LO) * CORES + core, "tm": (x * NY + y) * NZ_HI + z // NZ_LO}
+
+
+def table_peers(x, y, z, core):
+    base = (z // NEAR) * NEAR
+    return {
+        "core": [device(x, y, z, 1 - core)],
+        "x": [device(lax.rem(x + r, NX), y, z, core) for r in range(1, NX)],
+        "y": [device(x, lax.rem(y + r, NY), z, core) for r in range(1, NY)],
+        "far": [device(x, y, lax.rem(z + r * NEAR, NZ), core) for r in range(1, FAR)],
+        "near": [device(x, y, base + lax.rem(z - base + r, NEAR), core) for r in range(1, NEAR)],
+    }
+
+
 def kernel(
     length_ref, q_hbm, k_hbm, v_hbm, g_hbm, rel_ref,
     dq_hbm, dk_hbm, dv_hbm, table_ref,
@@ -64,7 +87,8 @@
     expo, dpr, toep, skew, dk_acc, dv_acc, dq_tr, dq_own, gmask,
     st_send, st_recv, bk_send, bk_recv, tops, parts,
     odq, odk, odv,
-    load_sem, out_sem, send_sem, recv_sem,
+    halves, other, slot_x, thirds, slot_y, slot_far, slot_near, gather_y, gather,
+    load_sem, out_sem, send_sem, recv_sem, sum_send, sum_recv,
 ):
     dp = lax.axis_index("dp")
     tm = lax.axis_index("tm")
@@ -114,9 +138,12 @@
         copy.start()
 
     barrier = pltpu.get_barrier_semaphore()
-    for neighbour in (before, after):
-        pl.semaphore_signal(barrier, inc=1, device_id=neighbour, device_id_type=MESH)
-    pl.semaphore_wait(barrier, 2)
+    x, y, z, core = place(dp, tm)
+    peers = table_peers(x, y, z, core)
+    partners = [before, after] + [peer for some in peers.values() for peer in some]
+    for partner in partners:
+        pl.semaphore_signal(barrier, inc=1, device_id=partner, device_id_type=MESH)
+    pl.semaphore_wait(barrier, len(partners))
     send_q(0).start()
     send_g(0).start()
 
@@ -181,10 +208,6 @@
         send_q(g).wait_recv()
         send_g(g).wait_recv()
         send_stats(g).wait_recv()
-
-        @pl.when(g > 0)
-        def _():
-            send_dq(g - 1).start()
 
         gmask[...] = jnp.where(
             frame_row < live_next, rg[g].astype(jnp.float32), 0.0
@@ -228,7 +251,8 @@
         return carry
 
     lax.fori_loop(0, groups, cross, 0)
-    send_dq(groups - 1).start()
+    for g in range(groups):
+        send_dq(g).start()
 
     def own_rest(g, carry):
         send_back(g).wait_recv()
@@ -258,7 +282,50 @@
     for bit in (1, 2, 4):
         folded = jnp.where(((7 - sub) & bit) != 0, pltpu.roll(folded, bit, 2), folded)
     sums = jnp.sum(folded, axis=1)
-    table_ref[...] = pltpu.roll(reverse_lanes(sums), 3 * BLOCK - 1, 1)
+    table = pltpu.roll(reverse_lanes(sums), 3 * BLOCK - 1, 1)
+
+    halves[0] = table[:8]
+    halves[1] = jnp.concatenate([table[8:], jnp.zeros((16 - heads, 3 * BLOCK), jnp.float32)], axis=0)
+
+    def swap(step, targets, src, dst):
+        copies = [
+            pltpu.make_async_remote_copy(
+                src_ref=src(r), dst_ref=dst,
+                send_sem=sum_send.at[step, r], recv_sem=sum_recv.at[step, r],
+                device_id=target, device_id_type=MESH,
+            )
+            for r, target in enumerate(targets)
+        ]
+        for copy in copies:
+            copy.start()
+        for copy in copies:
+            copy.wait()
+
+    def total(slots, count):
+        value = slots[0]
+        for n in range(1, count):
+            value = value + slots[n]
+        return value
+
+    def swap_slots(step, targets, slots, mine, value):
+        slots[mine] = value
+        swap(step, targets, lambda r: slots.at[mine], slots.at[mine])
+
+    swap(0, peers["core"], lambda r: halves.at[1 - core], other)
+    swap_slots(1, peers["x"], slot_x, x, halves[core] + other[...])
+    summed = total(slot_x, NX)
+    for n in range(3):
+        thirds[n] = summed[:, n * BLOCK : (n + 1) * BLOCK]
+    slot_y[y] = thirds[jnp.minimum(y, 2)]
+    swap(2, peers["y"], lambda r: thirds.at[jnp.minimum(lax.rem(y + r + 1, NY), 2)], slot_y.at[y])
+    swap_slots(3, peers["far"], slot_far, z // NEAR, total(slot_y, NY))
+    swap_slots(4, peers["near"], slot_near, z % NEAR, total(slot_far, FAR))
+    swap_slots(5, peers["y"], gather_y, y, total(slot_near, NEAR))
+    for n in range(3):
+        gather[core, :, n * BLOCK : (n + 1) * BLOCK] = gather_y[n]
+    swap(6, peers["core"], lambda r: gather.at[core], gather.at[core])
+    table_ref[:8, :] = gather[0]
+    table_ref[8:, :] = gather[1, : heads - 8, :]
 
     def finish(g, carry):
         send_dq(g).wait_recv()
@@ -285,7 +352,7 @@
     block = jax.ShapeDtypeStruct((1, frames, width), bf16)
     anywhere = pl.BlockSpec(memory_space=pl.ANY)
     in_vmem = pl.BlockSpec(memory_space=pltpu.VMEM)
-    dq, dk, dv, table = pl.pallas_call(
+    return pl.pallas_call(
         kernel,
         out_shape=(block, block, block, jax.ShapeDtypeStruct((heads, offsets), f32)),
         in_specs=[pl.BlockSpec(memory_space=pltpu.SMEM)] + [anywhere] * 4 + [in_vmem],
@@ -305,16 +372,26 @@
             stats, stats, stats, stats, stats,
             pltpu.VMEM((heads, 8, offsets), f32),
             wide, wide, wide,
+            pltpu.VMEM((2, 8, offsets), f32),
+            pltpu.VMEM((8, offsets), f32),
+            pltpu.VMEM((NX, 8, offsets), f32),
+            pltpu.VMEM((3, 8, BLOCK), f32),
+            pltpu.VMEM((NY, 8, BLOCK), f32),
+            pltpu.VMEM((FAR, 8, BLOCK), f32),
+            pltpu.VMEM((NEAR, 8, BLOCK), f32),
+            pltpu.VMEM((NY, 8, BLOCK), f32),
+            pltpu.VMEM((2, 8, offsets), f32),
             pltpu.SemaphoreType.DMA((4, groups)),
             pltpu.SemaphoreType.DMA((3, groups)),
             pltpu.SemaphoreType.DMA((5, groups)),
             pltpu.SemaphoreType.DMA((5, groups)),
+            pltpu.SemaphoreType.DMA((7, 3)),
+            pltpu.SemaphoreType.DMA((7, 3)),
         ],
         compiler_params=pltpu.CompilerParams(
-            collective_id=0, has_side_effects=True, vmem_limit_bytes=48 << 20
+            collective_id=0, has_side_effects=True, vmem_limit_bytes=60 << 20
         ),
     )(lengths, queries, keys, values, out_grad, rel_bias)
-    return dq, dk, dv, lax.psum(table, ("dp", "tm"))
 
 
 def solution(mesh):

time: 291 us -> 206 us (0.71)
  blocking collectives: 116 us -> 0 us
  Pallas kernels: 166 us -> 200 us
    psum x1 -> x0, blocking collectives: 116 us -> none  [per_device(): return (dq, dk, dv, lax.psum(table, ('dp', 'tm')))]
    pallas_call x1, Pallas kernels: 166 us -> 200 us  [per_device(): pl.pallas_call(kernel, out_shape=(block, block, block, jax.ShapeDtypeStru...]
    unnamed x13 -> x10, local copies, waits for them, and re-layouts: 7.49 us -> 4.7 us
where the time goes in v1:
time: 206 us
  Pallas kernels  200 us (97%)
  local copies, waits for them, and re-layouts  4.7 us (2%)
    pallas_call x1, Pallas kernels, per_device(): pl.pallas_call(kernel, out_shape=(block, block, block, jax.ShapeDtypeStru...  200 us
    unnamed x10, local copies, waits for them, and re-layouts  4.7 us

profile of v1, /device:TPU:1, one launch (start us, length us, event | category | flops | bytes accessed | tf_op | source)
XLA Modules:
  0.0 205.6 jit_solution(13828728509124988941)
XLA Ops:
  1.3 199.6 %shard_map.93 = (bf16[1,256,1152]{2,1,0:T(8,128)(2,1)}, bf16[1,256,1152]{2,1,0:T(8,128)(2,1)}, bf16[1,256,1152]{2,1,0:T(8,128)(2,1)}, f32[12,768]{1,0:T(8,128)}) custom-call(s32[1]{0:T(128)S(6)} %copy.14.length_ref, bf16[1,256,1152]{2,1,0:T(8,128)(2,1)} %q_hbm.1, bf16[1,256,1152]{2,1,0:T(8,128)(2,1)} %k_hbm.1, bf16[1,256,1152]{2,1,0:T(8,128)(2,1)} %v_hbm.1, ...), custom_call_target="tpu_custom_call" | custom-call | tf_op jit(solution)/shard_map/pallas_call | solution.py:355
  200.9 0.0 copy-start.1
  200.9 2.0 copy.15
  202.9 0.0 copy-done.1
  202.9 0.0 copy-start
  202.9 0.8 copy.16
  203.7 0.5 copy-done
  204.2 0.0 copy-start.2
  204.2 0.8 copy.17
  205.0 0.0 copy-done.2
  205.0 0.6 copy.18
Async XLA Ops:
  200.9 2.0 copy-start.1
  202.9 1.3 copy-start
  204.2 0.8 copy-start.2

commit v2 on v0

--- a/solution.py
+++ b/solution.py
@@ -13,6 +13,11 @@
 WIDE = GROUP * HEAD
 WINDOWS = ((0, 128), (0, 256), (128, 256), (256, 128))
 SCALING = HEAD ** (-0.5)
+HAND_ON = 2
+NX, NY, NZ_HI, NZ_LO, CORES = 4, 4, 2, 8, 2
+NZ = NZ_HI * NZ_LO
+COLUMNS = NX * NY
+TILES = 6
 
 
 def nt(a, b):
@@ -57,14 +62,24 @@
     return jnp.concatenate([zeros, x[0]], axis=1) + jnp.concatenate([x[1], zeros], axis=1)
 
 
+def place(dp, tm):
+    return tm // NZ_HI // NY, tm // NZ_HI % NY, (tm % NZ_HI) * NZ_LO + dp // CORES, dp % CORES
+
+
+def device(x, y, z, core):
+    return {"dp": (z % NZ_LO) * CORES + core, "tm": (x * NY + y) * NZ_HI + z // NZ_LO}
+
+
 def kernel(
     length_ref, q_hbm, k_hbm, v_hbm, g_hbm, rel_ref,
     dq_hbm, dk_hbm, dv_hbm, table_ref,
-    qbuf, kbuf, vbuf, gbuf, ktr, rq, rg, sdq, rdq,
+    qbuf, kbuf, vbuf, gbuf, glive, ktr, rq, rg, sdq, rdq,
     expo, dpr, toep, skew, dk_acc, dv_acc, dq_tr, dq_own, gmask,
     st_send, st_recv, bk_send, bk_recv, tops, parts,
     odq, odk, odv,
+    halves, other, tiles, slot_xy, slot_z, gather,
     load_sem, out_sem, send_sem, recv_sem,
+    core_send, core_recv, xy_send, xy_recv, z_send, z_recv, back_send, back_recv,
 ):
     dp = lax.axis_index("dp")
     tm = lax.axis_index("tm")
@@ -85,10 +100,10 @@
         )
 
     def send_q(g):
-        return remote(q_hbm.at[0, :, lanes(g)], rq, 0, g, before)
+        return remote(qbuf.at[g], rq, 0, g, before)
 
     def send_g(g):
-        return remote(g_hbm.at[0, :, lanes(g)], rg, 1, g, before)
+        return remote(gbuf.at[g], rg, 1, g, before)
 
     def send_stats(g):
         return remote(st_send.at[g], st_recv, 2, g, before)
@@ -114,9 +129,18 @@
         copy.start()
 
     barrier = pltpu.get_barrier_semaphore()
-    for neighbour in (before, after):
-        pl.semaphore_signal(barrier, inc=1, device_id=neighbour, device_id_type=MESH)
-    pl.semaphore_wait(barrier, 2)
+    x, y, z, core = place(dp, tm)
+    column = x * NY + y
+    partner_core = device(x, y, z, 1 - core)
+    around = [lax.rem(column + r, COLUMNS) for r in range(1, COLUMNS)]
+    around = [device(other_column // NY, other_column % NY, z, core) for other_column in around]
+    along = [device(x, y, lax.rem(z + r, NZ), core) for r in range(1, NZ)]
+    partners = [before, after, partner_core] + around + along
+    for partner in partners:
+        pl.semaphore_signal(barrier, inc=1, device_id=partner, device_id_type=MESH)
+    pl.semaphore_wait(barrier, len(partners))
+    for n in (0, 3):
+        loads[n].wait()
     send_q(0).start()
     send_g(0).start()
 
@@ -141,15 +165,16 @@
         return carry
 
     lax.fori_loop(0, heads, build, 0)
-    for copy in loads:
-        copy.wait()
+    for n, copy in enumerate(loads):
+        if n not in (0, 3):
+            copy.wait()
 
     key_row = lax.broadcasted_iota(jnp.int32, (BLOCK, BLOCK), 0)
     frame_row = lax.broadcasted_iota(jnp.int32, (BLOCK, WIDE), 0)
 
     def own_stats(g, carry):
         live = frame_row < live_keys
-        gbuf[g] = jnp.where(live, gbuf[g].astype(jnp.float32), 0.0).astype(jnp.bfloat16)
+        glive[g] = jnp.where(live, gbuf[g].astype(jnp.float32), 0.0).astype(jnp.bfloat16)
         ktr[g] = kbuf[g].T
         for j in range(GROUP):
             h = g * GROUP + j
@@ -161,7 +186,7 @@
             scores = jnp.where(key_row < live_keys, scores, MASKED)
             top = jnp.max(scores, axis=0, keepdims=True)
             e = jnp.exp(scores - top)
-            dprobs = nt(vbuf[g, :, window] * mask, gbuf[g, :, window])
+            dprobs = nt(vbuf[g, :, window] * mask, glive[g, :, window])
             total = jnp.sum(e, axis=0, keepdims=True)
             mixed = jnp.sum(e * dprobs, axis=0, keepdims=True)
             expo[h] = e
@@ -177,14 +202,10 @@
         send_q(g).start()
         send_g(g).start()
 
-    def cross(g, carry):
+    def cross(g):
         send_q(g).wait_recv()
         send_g(g).wait_recv()
         send_stats(g).wait_recv()
-
-        @pl.when(g > 0)
-        def _():
-            send_dq(g - 1).start()
 
         gmask[...] = jnp.where(
             frame_row < live_next, rg[g].astype(jnp.float32), 0.0
@@ -225,12 +246,8 @@
             parts[h, :, BLOCK:] = diagonal_partials(dscores)
         send_back(g).start()
         sdq[g] = (dq_tr[...].T * SCALING).astype(jnp.bfloat16)
-        return carry
-
-    lax.fori_loop(0, groups, cross, 0)
-    send_dq(groups - 1).start()
-
-    def own_rest(g, carry):
+
+    def own_rest(g):
         send_back(g).wait_recv()
         for j in range(GROUP):
             h = g * GROUP + j
@@ -241,7 +258,7 @@
             dscores = probs * (dpr[h] - bk_recv[g, GROUP + j : GROUP + j + 1, :])
             probs_b = probs.astype(jnp.bfloat16)
             dscores_b = dscores.astype(jnp.bfloat16)
-            dv_acc[g, :, window] += nn(probs_b, gbuf[g, :, window] * mask)
+            dv_acc[g, :, window] += nn(probs_b, glive[g, :, window] * mask)
             dk_acc[g, :, window] += nn(dscores_b, qbuf[g, :, window] * mask)
             dq_tr[HEAD * j : HEAD * (j + 1), :] = nn(ktr[g, HEAD * j : HEAD * (j + 1), :], dscores_b)
             parts[h, :, : 2 * BLOCK] += diagonal_partials(dscores)
@@ -250,15 +267,113 @@
         odv[g] = dv_acc[g].astype(jnp.bfloat16)
         store(1, odk, dk_hbm, g).start()
         store(2, odv, dv_hbm, g).start()
+
+    def step(g, carry):
+        @pl.when(g < groups)
+        def _():
+            cross(g)
+
+        @pl.when(g == groups - 1)
+        def _():
+            for n in range(groups):
+                send_dq(n).start()
+
+        @pl.when(g > 0)
+        def _():
+            own_rest(g - 1)
+
         return carry
 
-    lax.fori_loop(0, groups, own_rest, 0)
+    lax.fori_loop(0, groups + 1, step, 0)
 
     folded = parts[...]
     for bit in (1, 2, 4):
         folded = jnp.where(((7 - sub) & bit) != 0, pltpu.roll(folded, bit, 2), folded)
     sums = jnp.sum(folded, axis=1)
-    table_ref[...] = pltpu.roll(reverse_lanes(sums), 3 * BLOCK - 1, 1)
+    table = pltpu.roll(reverse_lanes(sums), 3 * BLOCK - 1, 1)
+
+    padded = jnp.concatenate([table, jnp.zeros((16 - heads, 3 * BLOCK), jnp.float32)], axis=0)
+    for c in range(2):
+        for k in range(TILES):
+            halves[c, k] = padded[8 * c : 8 * c + 8, 128 * k : 128 * k + 128]
+
+    def move(src, dst, send, recv, target):
+        return pltpu.make_async_remote_copy(
+            src_ref=src, dst_ref=dst, send_sem=send, recv_sem=recv, device_id=target, device_id_type=MESH
+        )
+
+    swap = move(halves.at[1 - core], other, core_send.at[0], core_recv.at[0], partner_core)
+    swap.start()
+    swap.wait()
+    tiles[...] = halves[core] + other[...]
+
+    def to_owner(k):
+        owner = device(k // NY, k % NY, z, core)
+        return move(tiles.at[k], slot_xy.at[column], xy_send.at[k], xy_recv.at[column], owner)
+
+    def from_column(c):
+        return move(tiles.at[0], slot_xy.at[c], xy_send.at[0], xy_recv.at[c], partner_core)
+
+    def to_z(r):
+        return move(slot_z.at[z], slot_z.at[z], z_send.at[r], z_recv.at[r], along[r])
+
+    def to_column(c):
+        target = device(c // NY, c % NY, z, core)
+        mine = gather.at[core, column]
+        return move(mine, mine, back_send.at[c], back_recv.at[column], target)
+
+    def from_owner(k):
+        part = gather.at[core, k]
+        return move(part, part, back_send.at[0], back_recv.at[k], partner_core)
+
+    for k in range(TILES):
+        @pl.when(column != k)
+        def _():
+            to_owner(k).start()
+
+    @pl.when(column < TILES)
+    def _():
+        slot_xy[column] = tiles[column]
+        for c in range(COLUMNS):
+            @pl.when(column != c)
+            def _():
+                from_column(c).wait_recv()
+        value = slot_xy[0]
+        for c in range(1, COLUMNS):
+            value = value + slot_xy[c]
+        slot_z[z] = value
+        for r in range(NZ - 1):
+            to_z(r).start()
+        for r in range(NZ - 1):
+            to_z(r).wait()
+        value = slot_z[0]
+        for n in range(1, NZ):
+            value = value + slot_z[n]
+        gather[core, column] = value
+        for c in range(COLUMNS):
+            @pl.when(column != c)
+            def _():
+                to_column(c).start()
+
+    for k in range(TILES):
+        @pl.when(column != k)
+        def _():
+            from_owner(k).wait_recv()
+            to_owner(k).wait_send()
+
+    @pl.when(column < TILES)
+    def _():
+        for c in range(COLUMNS):
+            @pl.when(column != c)
+            def _():
+                to_column(c).wait_send()
+
+    swap = move(gather.at[core], gather.at[core], core_send.at[1], core_recv.at[1], partner_core)
+    swap.start()
+    swap.wait()
+    for k in range(TILES):
+        table_ref[:8, 128 * k : 128 * k + 128] = gather[0, k]
+        table_ref[8:, 128 * k : 128 * k + 128] = gather[1, k, : heads - 8, :]
 
     def finish(g, carry):
         send_dq(g).wait_recv()
@@ -272,6 +387,13 @@
             copy.wait_send()
         for n, (src, dst) in enumerate(((odq, dq_hbm), (odk, dk_hbm), (odv, dv_hbm))):
             store(n, src, dst, g).wait()
+
+
+def hand_on(dq, dk, dv, table, dq_out, dk_out, dv_out, table_out):
+    dq_out[...] = dq[...]
+    dk_out[...] = dk[...]
+    dv_out[...] = dv[...]
+    table_out[...] = table[...]
 
 
 def per_device(queries, keys, values, out_grad, lengths, rel_bias):
@@ -285,13 +407,13 @@
     block = jax.ShapeDtypeStruct((1, frames, width), bf16)
     anywhere = pl.BlockSpec(memory_space=pl.ANY)
     in_vmem = pl.BlockSpec(memory_space=pltpu.VMEM)
-    dq, dk, dv, table = pl.pallas_call(
+    results = pl.pallas_call(
         kernel,
         out_shape=(block, block, block, jax.ShapeDtypeStruct((heads, offsets), f32)),
         in_specs=[pl.BlockSpec(memory_space=pltpu.SMEM)] + [anywhere] * 4 + [in_vmem],
         out_specs=(anywhere, anywhere, anywhere, in_vmem),
         scratch_shapes=[
-            wide, wide, wide, wide,
+            wide, wide, wide, wide, wide,
             pltpu.VMEM((groups, WIDE, BLOCK), bf16),
             wide, wide, wide, wide,
             pltpu.VMEM((heads, BLOCK, BLOCK), f32),
@@ -305,16 +427,39 @@
             stats, stats, stats, stats, stats,
             pltpu.VMEM((heads, 8, offsets), f32),
             wide, wide, wide,
+            pltpu.VMEM((2, TILES, 8, 128), f32),
+            pltpu.VMEM((TILES, 8, 128), f32),
+            pltpu.VMEM((TILES, 8, 128), f32),
+            pltpu.VMEM((COLUMNS, 8, 128), f32),
+            pltpu.VMEM((NZ, 8, 128), f32),
+            pltpu.VMEM((2, TILES, 8, 128), f32),
             pltpu.SemaphoreType.DMA((4, groups)),
             pltpu.SemaphoreType.DMA((3, groups)),
             pltpu.SemaphoreType.DMA((5, groups)),
             pltpu.SemaphoreType.DMA((5, groups)),
+            pltpu.SemaphoreType.DMA((2,)),
+            pltpu.SemaphoreType.DMA((2,)),
+            pltpu.SemaphoreType.DMA((TILES,)),
+            pltpu.SemaphoreType.DMA((COLUMNS,)),
+            pltpu.SemaphoreType.DMA((NZ,)),
+            pltpu.SemaphoreType.DMA((NZ,)),
+            pltpu.SemaphoreType.DMA((COLUMNS,)),
+            pltpu.SemaphoreType.DMA((TILES,)),
         ],
         compiler_params=pltpu.CompilerParams(
-            collective_id=0, has_side_effects=True, vmem_limit_bytes=48 << 20
+            collective_id=0, has_side_effects=True, vmem_limit_bytes=60 << 20
         ),
     )(lengths, queries, keys, values, out_grad, rel_bias)
-    return dq, dk, dv, lax.psum(table, ("dp", "tm"))
+    rows = pl.BlockSpec((1, frames // HAND_ON, width), lambda i: (0, i, 0))
+    whole = pl.BlockSpec((heads, offsets), lambda i: (0, 0))
+    return pl.pallas_call(
+        hand_on,
+        grid=(HAND_ON,),
+        out_shape=(block, block, block, jax.ShapeDtypeStruct((heads, offsets), f32)),
+        in_specs=[rows, rows, rows, whole],
+        out_specs=(rows, rows, rows, whole),
+        compiler_params=pltpu.CompilerParams(vmem_limit_bytes=60 << 20),
+    )(*results)
 
 
 def solution(mesh):

time: 291 us -> 202 us (0.69)
  blocking collectives: 116 us -> 0 us
  Pallas kernels: 166 us -> 201 us
  local copies, waits for them, and re-layouts: 7.49 us -> 0 us
    psum x1 -> x0, blocking collectives: 116 us -> none  [per_device(): return (dq, dk, dv, lax.psum(table, ('dp', 'tm')))]
    pallas_call x1, Pallas kernels: 166 us -> 198 us  [per_device(): pl.pallas_call(kernel, out_shape=(block, block, block, jax.ShapeDtypeStru...]
    unnamed x13 -> x0, local copies, waits for them, and re-layouts: 7.49 us -> none
where the time goes in v2:
time: 202 us
  Pallas kernels  201 us (100%)
    pallas_call x1, Pallas kernels, per_device(): pl.pallas_call(kernel, out_shape=(block, block, block, jax.ShapeDtypeStru...  198 us

profile of v2, /device:TPU:1, one launch (start us, length us, event | category | flops | bytes accessed | tf_op | source)
XLA Modules:
  0.0 201.8 jit_solution(5726392872983585666)
XLA Ops:
  1.3 198.1 %shard_map.93 = (bf16[1,256,1152]{2,1,0:T(8,128)(2,1)}, bf16[1,256,1152]{2,1,0:T(8,128)(2,1)}, bf16[1,256,1152]{2,1,0:T(8,128)(2,1)}, f32[12,768]{1,0:T(8,128)}) custom-call(s32[1]{0:T(128)S(6)} %copy.10.length_ref, bf16[1,256,1152]{2,1,0:T(8,128)(2,1)} %q_hbm.1, bf16[1,256,1152]{2,1,0:T(8,128)(2,1)} %k_hbm.1, bf16[1,256,1152]{2,1,0:T(8,128)(2,1)} %v_hbm.1, ...), custom_call_target="tpu_custom_call" | custom-call | tf_op jit(solution)/shard_map/pallas_call | solution.py:410
  199.3 2.5 %shard_map.94 = (bf16[1,256,1152]{2,1,0:T(8,128)(2,1)}, bf16[1,256,1152]{2,1,0:T(8,128)(2,1)}, bf16[1,256,1152]{2,1,0:T(8,128)(2,1)}, f32[12,768]{1,0:T(8,128)}) custom-call(bf16[1,256,1152]{2,1,0:T(8,128)(2,1)} %get-tuple-element.8.dq, bf16[1,256,1152]{2,1,0:T(8,128)(2,1)} %get-tuple-element.9.dk, bf16[1,256,1152]{2,1,0:T(8,128)(2,1)} %get-tuple-element.10.dv, ...), custom_call_target="tpu_custom_call" | custom-call | tf_op jit(solution)/shard_map/pallas_call | solution.py:455

commit v3 on v2

--- a/solution.py
+++ b/solution.py
@@ -74,7 +74,7 @@
     length_ref, q_hbm, k_hbm, v_hbm, g_hbm, rel_ref,
     dq_hbm, dk_hbm, dv_hbm, table_ref,
     qbuf, kbuf, vbuf, gbuf, glive, ktr, rq, rg, sdq, rdq,
-    expo, dpr, toep, skew, dk_acc, dv_acc, dq_tr, dq_own, gmask,
+    expo, dpr, cross_expo, cross_dpr, shift, toep, skew, dk_acc, dv_acc, dq_tr, dq_own, gmask,
     st_send, st_recv, bk_send, bk_recv, tops, parts,
     odq, odk, odv,
     halves, other, tiles, slot_xy, slot_z, gather,
@@ -113,6 +113,14 @@
 
     def send_dq(g):
         return remote(sdq.at[g], rdq, 4, g, after)
+
+    def send_first(r):
+        rows = pl.ds(r * (BLOCK // 2), BLOCK // 2)
+        return pltpu.make_async_remote_copy(
+            src_ref=sdq.at[0, rows], dst_ref=rdq.at[0, rows],
+            send_sem=send_sem.at[5, r], recv_sem=recv_sem.at[5, r],
+            device_id=after, device_id_type=MESH,
+        )
 
     def load(n, src, dst, g):
         return pltpu.make_async_copy(src.at[0, :, lanes(g)], dst.at[g], load_sem.at[n, g])
@@ -235,8 +243,25 @@
             delta = (here * (mixed / total) + there * st_recv[g, GROUP + j : GROUP + j + 1, :]) / both
             bk_send[g, j : j + 1, :] = lse
             bk_send[g, GROUP + j : GROUP + j + 1, :] = delta
-            probs = e * jnp.exp(top - lse)
-            dscores = probs * (dprobs - delta)
+            shift[j : j + 1, :] = top - lse
+            cross_expo[j] = e
+            cross_dpr[j] = dprobs
+        send_back(g).start()
+
+        @pl.when(g == groups - 1)
+        def _():
+            send_first(1).start()
+            for n in range(1, groups - 1):
+                send_dq(n).start()
+
+        for j in range(GROUP):
+            h = g * GROUP + j
+            start, width = WINDOWS[j]
+            window = slice(start, start + width)
+            mask = head_lanes(j)
+            delta = bk_send[g, GROUP + j : GROUP + j + 1, :]
+            probs = cross_expo[j] * jnp.exp(shift[j : j + 1, :])
+            dscores = probs * (cross_dpr[j] - delta)
             probs_b = probs.astype(jnp.bfloat16)
             dscores_b = dscores.astype(jnp.bfloat16)
             dv_acc[g, :, window] += nn(probs_b, gmask[:, window] * mask)
@@ -244,8 +269,11 @@
             dq_tr[HEAD * j : HEAD * (j + 1), :] = nn(ktr[g, HEAD * j : HEAD * (j + 1), :], dscores_b)
             parts[h, :, : BLOCK] = jnp.zeros((8, BLOCK), jnp.float32)
             parts[h, :, BLOCK:] = diagonal_partials(dscores)
-        send_back(g).start()
         sdq[g] = (dq_tr[...].T * SCALING).astype(jnp.bfloat16)
+
+        @pl.when(g == 0)
+        def _():
+            send_first(0).start()
 
     def own_rest(g):
         send_back(g).wait_recv()
@@ -275,8 +303,7 @@
 
         @pl.when(g == groups - 1)
         def _():
-            for n in range(groups):
-                send_dq(n).start()
+            send_dq(groups - 1).start()
 
         @pl.when(g > 0)
         def _():
@@ -376,14 +403,24 @@
         table_ref[8:, 128 * k : 128 * k + 128] = gather[1, k, : heads - 8, :]
 
     def finish(g, carry):
-        send_dq(g).wait_recv()
+        @pl.when(g == 0)
+        def _():
+            for r in range(2):
+                send_first(r).wait_recv()
+
+        @pl.when(g > 0)
+        def _():
+            send_dq(g).wait_recv()
+
         odq[g] = (dq_own[g] + rdq[g].astype(jnp.float32)).astype(jnp.bfloat16)
         store(0, odq, dq_hbm, g).start()
         return carry
 
     lax.fori_loop(0, groups, finish, 0)
     for g in range(groups):
-        for copy in (send_q(g), send_g(g), send_stats(g), send_back(g), send_dq(g)):
+        for copy in (send_q(g), send_g(g), send_stats(g), send_back(g)):
+            copy.wait_send()
+        for copy in (send_first(0), send_first(1)) if g == 0 else (send_dq(g),):
             copy.wait_send()
         for n, (src, dst) in enumerate(((odq, dq_hbm), (odk, dk_hbm), (odv, dv_hbm))):
             store(n, src, dst, g).wait()
@@ -418,6 +455,9 @@
             wide, wide, wide, wide,
             pltpu.VMEM((heads, BLOCK, BLOCK), f32),
             pltpu.VMEM((heads, BLOCK, BLOCK), f32),
+            pltpu.VMEM((GROUP, BLOCK, BLOCK), f32),
+            pltpu.VMEM((GROUP, BLOCK, BLOCK), f32),
+            pltpu.VMEM((2 * GROUP, BLOCK), f32),
             pltpu.VMEM((heads, BLOCK, 2 * BLOCK), f32),
             pltpu.VMEM((heads, 8, offsets), f32),
             wide32, wide32,
@@ -435,8 +475,8 @@
             pltpu.VMEM((2, TILES, 8, 128), f32),
             pltpu.SemaphoreType.DMA((4, groups)),
             pltpu.SemaphoreType.DMA((3, groups)),
-            pltpu.SemaphoreType.DMA((5, groups)),
-            pltpu.SemaphoreType.DMA((5, groups)),
+            pltpu.SemaphoreType.DMA((6, groups)),
+            pltpu.SemaphoreType.DMA((6, groups)),
             pltpu.SemaphoreType.DMA((2,)),
             pltpu.SemaphoreType.DMA((2,)),
             pltpu.SemaphoreType.DMA((TILES,)),

time: 202 us -> 202 us (level)
  no operation moved by 1% of the time
where the time goes in v3:
time: 202 us; the launch traced here: 201 us
  Pallas kernels  200 us (99%)
    pallas_call x1, Pallas kernels, per_device(): pl.pallas_call(kernel, out_shape=(block, block, block, jax.ShapeDtypeStru...  198 us

profile of v3, /device:TPU:1, one launch (start us, length us, event | category | flops | bytes accessed | tf_op | source)
XLA Modules:
  0.0 201.4 jit_solution(10602292441072682236)
XLA Ops:
  1.3 197.7 %shard_map.93 = (bf16[1,256,1152]{2,1,0:T(8,128)(2,1)}, bf16[1,256,1152]{2,1,0:T(8,128)(2,1)}, bf16[1,256,1152]{2,1,0:T(8,128)(2,1)}, f32[12,768]{1,0:T(8,128)}) custom-call(s32[1]{0:T(128)S(6)} %copy.10.length_ref, bf16[1,256,1152]{2,1,0:T(8,128)(2,1)} %q_hbm.1, bf16[1,256,1152]{2,1,0:T(8,128)(2,1)} %k_hbm.1, bf16[1,256,1152]{2,1,0:T(8,128)(2,1)} %v_hbm.1, ...), custom_call_target="tpu_custom_call" | custom-call | tf_op jit(solution)/shard_map/pallas_call | solution.py:447
  199.0 2.5 %shard_map.94 = (bf16[1,256,1152]{2,1,0:T(8,128)(2,1)}, bf16[1,256,1152]{2,1,0:T(8,128)(2,1)}, bf16[1,256,1152]{2,1,0:T(8,128)(2,1)}, f32[12,768]{1,0:T(8,128)}) custom-call(bf16[1,256,1152]{2,1,0:T(8,128)(2,1)} %get-tuple-element.8.dq, bf16[1,256,1152]{2,1,0:T(8,128)(2,1)} %get-tuple-element.9.dk, bf16[1,256,1152]{2,1,0:T(8,128)(2,1)} %get-tuple-element.10.dv, ...), custom_call_target="tpu_custom_call" | custom-call | tf_op jit(solution)/shard_map/pallas_call | solution.py:495
